TPU v7x, 32 devices: a whole 2x2x4 slice. The times are simulated.
32 devices in a mesh: lat: 8 (over z, core), lon: 4 (over y, x).
Axes of the slice: x: 2, y: 2, z: 4, core: 2. Of those that a mesh axis runs over, the one named last changes fastest.
Arguments:
- queries: bfloat16 [16, 256, 2048], P('lat', 'lon'), may hold values from -50 to 50
- keyval: bfloat16 [2, 16, 256, 2048], P(None, 'lat', 'lon'), may hold values from -5 to 5
- keep: int32 [16], replicated, may hold values from 0 to 1, as said below
- lists: int32 [16, 8, 13], P('lat', 'lon'), may hold values from 0 to 14, as said below
Outputs:
- attended: bfloat16 [16, 256, 2048], P('lat', 'lon')
- gram_factor: float32 [8, 16, 128, 128], P('lat')
Inputs may be any that keep to these rules, and one draw needn't show every extreme that they name: `lists`: each list holds 13 different candidate numbers; its first is 7, the query block itself. keep is 0 in rows 0 and 15, and 1 outside the first and last 4 rows.
All inputs are finite; a program needn't handle non-finite values.
Results may differ from a plain program's by a relative error of at most 0.015.
Values may be sent and summed in bfloat16 or wider, within the bound.
A program may use at most 64 MiB of HBM per device.

v0:
```python
import jax
import jax.numpy as jnp
from jax import lax
from jax.sharding import PartitionSpec as P

HEADS = 16
HD = 128
BLOCK = 32
HALO = 2
CAND = 15


def extended(x, sides, width):
    for axis, dim in sides:
        size, length = (lax.axis_size(axis), x.shape[dim])
        up = [(i, (i + 1) % size) for i in range(size - 1)]
        down = [(j, i) for i, j in up]
        last = lax.slice_in_dim(x, length - width, length, axis=dim)
        leading = lax.slice_in_dim(x, 0, width, axis=dim)
        before = lax.ppermute(last, axis, up)
        after = lax.ppermute(leading, axis, down)
        x = jnp.concatenate([before, x, after], axis=dim)
    return x


def from_behind(x, axis, by):
    length = lax.axis_size(axis)
    return lax.ppermute(x, axis, [(i, (i + by) % length) for i in range(length)])


def visible_blocks(keep, lists, tile_rows):
    first_row = lax.axis_index("lat") * tile_rows
    total_rows = tile_rows * lax.axis_size("lat")
    padded = jnp.pad(keep, (HALO, HALO))
    local_keep = lax.dynamic_slice_in_dim(padded, first_row, tile_rows + 2 * HALO)
    ext_rows = (
        jnp.arange(tile_rows, dtype=jnp.int32)[:, None]
        + jnp.arange(2 * HALO + 1, dtype=jnp.int32)[None, :]
    )
    global_row = first_row + ext_rows - HALO
    inside = (global_row >= 0) & (global_row < total_rows)
    centre = (jnp.arange(2 * HALO + 1) == HALO)[None, :]
    row_ok = inside & (centre | (local_keep[ext_rows] == 1))
    listed = jnp.any(lists[..., None] == jnp.arange(CAND, dtype=jnp.int32), axis=2)
    return listed & jnp.repeat(row_ok, 3, axis=1)[:, None, :]


def local(queries, keyval, keep, lists):
    tile_rows, tile_cols, features = queries.shape
    blocks = tile_cols // BLOCK
    tall_band = extended(keyval, (("lat", 1),), HALO)
    west_keys = from_behind(tall_band[:, :, tile_cols - BLOCK :], "lon", 1)
    east_keys = from_behind(tall_band[:, :, :BLOCK], "lon", -1)
    wide_band = jnp.concatenate([west_keys, tall_band, east_keys], axis=2)
    wide_band = wide_band.reshape(2, tile_rows + 2 * HALO, blocks + 2, BLOCK, HEADS, HD)
    qblocks = queries.reshape(tile_rows, blocks, BLOCK, HEADS, HD)
    allowed = visible_blocks(keep, lists, tile_rows)
    gathered = []
    for offset in range(2 * HALO + 1):
        for lon_step in range(3):
            gathered.append(wide_band[:, offset : offset + tile_rows, lon_step : lon_step + blocks])
    cand_band = jnp.concatenate(gathered, axis=3)
    scores = jnp.einsum(
        "tbqhe,tbkhe->tbhqk", qblocks, cand_band[0], preferred_element_type=jnp.float32
    ) * HD ** (-0.5)
    key_mask = jnp.repeat(allowed, BLOCK, axis=2)[:, :, None, None, :]
    scores = jnp.where(key_mask, scores, -jnp.inf)
    row_top = jnp.max(scores, axis=-1, keepdims=True)
    weights = jnp.exp(scores - row_top)
    denominator = jnp.sum(weights, axis=-1)
    rounded = weights.astype(jnp.bfloat16)
    mixture = jnp.einsum(
        "tbhqk,tbkhe->tbqhe", rounded, cand_band[1], preferred_element_type=jnp.float32
    )
    attended = (mixture / jnp.transpose(denominator, (0, 1, 3, 2))[..., None]).astype(jnp.bfloat16)
    flat_rows = attended.reshape(tile_rows * tile_cols, HEADS, HD)
    partial_value = jnp.einsum(
        "nhd,nhe->hde", flat_rows, flat_rows, preferred_element_type=jnp.float32
    )
    gram_sum = lax.psum(partial_value.astype(jnp.bfloat16), "lon").astype(jnp.float32)
    return (attended.reshape(tile_rows, tile_cols, features), gram_sum[None])


def solution(mesh):
    placed = (P("lat", "lon", None), P(None, "lat", "lon", None), P(), P("lat", "lon", None))
    return jax.shard_map(
        local,
        mesh=mesh,
        in_specs=placed,
        out_specs=(P("lat", "lon", None), P("lat", None, None, None)),
        check_vma=False,
    )
```

profile of v0, /device:TPU:1, one launch (start us, length us, event | category | flops | bytes accessed | tf_op | source)
XLA Modules:
  0.0 190.0 jit_solution(7488668933029883605)
XLA Ops:
  7.2 0.0 copy-start.3
  7.2 0.0 copy-start.2
  7.2 0.0 all-reduce.3.cloned.1.call-start
  7.2 4.6 %collective-permute-start = (bf16[2,2,64,2048]{3,2,1,0:T(8,128)(2,1)}, bf16[2,2,64,2048]{3,2,1,0:T(8,128)(2,1)S(1)}, u32[]{:S(2)}, u32[]{:S(2)}) collective-permute-start(bf16[2,2,64,2048]{3,2,1,0:T(8,128)(2,1)} %param.5), channel_id=1, source_target_pairs={{0,4},{4,8},{8,12},{12,16},{16,20},{20,24},{24,28},{1,5},{5,9},{9,... | collective-permute-start | bytes 3145736 | tf_op jit(solution)/shard_map/ppermute | solution.py:20
  11.8 1.9 %collective-permute-start.1 = (bf16[2,2,64,2048]{3,2,1,0:T(8,128)(2,1)}, bf16[2,2,64,2048]{3,2,1,0:T(8,128)(2,1)S(1)}, u32[]{:S(2)}, u32[]{:S(2)}) collective-permute-start(bf16[2,2,64,2048]{3,2,1,0:T(8,128)(2,1)} %param.5), channel_id=1, source_target_pairs={{4,0},{8,4},{12,8},{16,12},{20,16},{24,20},{28,24},{5,1},{9,5},{13... | collective-permute-start | bytes 3145736 | tf_op jit(solution)/shard_map/ppermute | solution.py:21
  13.8 10.1 %collective-permute-done = bf16[2,2,64,2048]{3,2,1,0:T(8,128)(2,1)S(1)} collective-permute-done((bf16[2,2,64,2048]{3,2,1,0:T(8,128)(2,1)}, bf16[2,2,64,2048]{3,2,1,0:T(8,128)(2,1)S(1)}, u32[]{:S(2)}, u32[]{:S(2)}) %collective-permute-start) | collective-permute-done | bytes 1048608 | tf_op jit(solution)/shard_map/ppermute | solution.py:20
  23.9 0.1 constant_dynamic-update-slice_fusion.2
  24.0 1.3 constant_dynamic-update-slice_fusion.1
  25.3 3.3 %collective-permute-done.1 = bf16[2,2,64,2048]{3,2,1,0:T(8,128)(2,1)S(1)} collective-permute-done((bf16[2,2,64,2048]{3,2,1,0:T(8,128)(2,1)}, bf16[2,2,64,2048]{3,2,1,0:T(8,128)(2,1)S(1)}, u32[]{:S(2)}, u32[]{:S(2)}) %collective-permute-start.1) | collective-permute-done | bytes 1048608 | tf_op jit(solution)/shard_map/ppermute | solution.py:21
  28.6 0.1 constant_dynamic-update-slice_fusion
  28.7 1.9 fusion.26
  30.5 1.2 collective-permute-start.2
  31.8 1.2 collective-permute-start.3
  32.9 0.1 reshape.56
  33.0 0.0 copy-done.3
  33.0 0.1 pad_dynamic-slice_fusion
  33.1 0.7 gather_fusion
  33.8 0.1 reshape.64
  33.9 0.1 broadcast_in_dim.34
  33.9 0.1 and.19
  34.0 0.0 copy-done.2
  34.0 0.1 fusion.22
  34.2 0.1 broadcast_in_dim.35
  34.2 0.1 broadcast_in_dim.36
  34.3 2.0 %copy.64 = bf16[16,8,16,128]{3,2,1,0:T(8,128)(2,1)} copy(bf16[16,8,16,128]{3,1,2,0:T(8,128)(2,1)} %bitcast.56) | data formatting | bytes 1048576
  36.3 31.7 %collective-permute-done.2 = bf16[2,6,32,2048]{3,2,1,0:T(8,128)(2,1)} collective-permute-done((bf16[2,6,32,2048]{3,2,1,0:T(8,128)(2,1)}, bf16[2,6,32,2048]{3,2,1,0:T(8,128)(2,1)}, u32[]{:S(2)}, u32[]{:S(2)}) %collective-permute-start.2) | collective-permute-done | bytes 1572896 | tf_op jit(solution)/shard_map/ppermute | solution.py:28
  67.9 22.2 %collective-permute-done.3 = bf16[2,6,32,2048]{3,2,1,0:T(8,128)(2,1)} collective-permute-done((bf16[2,6,32,2048]{3,2,1,0:T(8,128)(2,1)}, bf16[2,6,32,2048]{3,2,1,0:T(8,128)(2,1)}, u32[]{:S(2)}, u32[]{:S(2)}) %collective-permute-start.3) | collective-permute-done | bytes 1572896 | tf_op jit(solution)/shard_map/ppermute | solution.py:28
  90.2 2.8 %pad_maximum_fusion = bf16[2,6,128,2048]{3,2,1,0:T(8,128)(2,1)S(1)} fusion(bf16[2,6,32,2048]{3,2,1,0:T(8,128)(2,1)} %collective-permute-done.3, bf16[2,6,64,2048]{3,2,1,0:T(8,128)(2,1)S(1)} %constant_dynamic-update-slice_fusion, bf16[2,6,32,2048]{3,2,1,0:T(8,128)(2,1)} %collective-permute-done.2), kind=kLoop, calls=%fused_computation.5 | loop fusion | flops 18874368 | bytes 12582912 | tf_op jit(solution)/shard_map/concatenate | solution.py:54
  92.9 2.3 %copy.63 = bf16[192,8,16,128]{3,2,1,0:T(8,128)(2,1)S(1)} copy(bf16[192,8,16,128]{3,1,2,0:T(8,128)(2,1)S(1)} %bitcast.54) | data formatting | bytes 12582912
  95.3 6.2 %fusion.25 = (bf16[2,2,2,32,16,128]{5,4,3,2,1,0:T(8,128)(2,1)S(1)}, bf16[2,2,2,32,16,128]{5,4,3,2,1,0:T(8,128)(2,1)S(1)}, bf16[2,2,2,32,16,128]{5,4,3,2,1,0:T(8,...) fusion(bf16[2,6,4,32,16,128]{5,4,3,2,1,0:T(8,128)(2,1)S(1)} %bi, ...), kind=kLoop, calls=%fused_computation.52 | loop fusion | bytes 31457280 | tf_op jit(solution)/shard_map/slice | solution.py:61
  101.5 0.3 copy_dynamic-update-slice_fusion.14
  101.8 0.3 copy_dynamic-update-slice_fusion.13
  102.1 0.3 copy_dynamic-update-slice_fusion.12
  102.5 0.3 copy_dynamic-update-slice_fusion.11
  102.8 0.3 copy_dynamic-update-slice_fusion.10
  103.2 0.3 copy_dynamic-update-slice_fusion.9
  103.5 0.3 copy_dynamic-update-slice_fusion.8
  103.9 0.3 copy_dynamic-update-slice_fusion.7
  104.2 0.0 copy-start
  104.2 0.3 copy_dynamic-update-slice_fusion.6
  104.6 0.3 copy_dynamic-update-slice_fusion.5
  104.9 0.3 copy_dynamic-update-slice_fusion.4
  105.3 0.3 copy_dynamic-update-slice_fusion.3
  105.6 0.3 copy_dynamic-update-slice_fusion.2
  106.0 0.3 copy_dynamic-update-slice_fusion.1
  106.3 0.3 copy_dynamic-update-slice_fusion
  106.7 0.0 copy-start.1
  106.7 5.5 %copy-done.1 = bf16[2,2,2,480,16,128]{5,3,4,2,1,0:T(8,128)(2,1)} copy-done((bf16[2,2,2,480,16,128]{5,3,4,2,1,0:T(8,128)(2,1)}, bf16[2,2,2,480,16,128]{5,3,4,2,1,0:T(8,128)(2,1)S(1)}, u32[]{:S(2)}) %copy-start.1) | copy-done | bytes 15728664
  112.2 0.0 copy-done
  112.2 6.4 %bitcast_reduce_fusion = (f32[2,2,16,32]{3,2,1,0:T(8,128)S(1)}, f32[2,2,16,480,32]{3,4,2,1,0:T(8,128)S(1)}) fusion(pred[2,2,480]{2,1,0:T(4,128)(4,1)S(1)} %broadcast_in_dim.36, bf16[2,2,32,16,128]{4,3,2,1,0:T(8,128)(2,1)S(1)} %bitcast.57, bf16[2,2,2,480,16,128]{5,3,4,2,1,0:T(8,128)(2,1)} %copy-done.1), kind=kOutput, calls=%fused_computation.7 | convolution fusion | flops 254605312 | bytes 12330880 | tf_op jit(solution)/shard_map/tbqhe,tbkhe->tbhqk/dot_general | solution.py:63
  118.6 1.3 fusion.3
  120.0 5.3 %fusion.17 = bf16[2,2,32,16,128]{4,2,3,1,0:T(8,128)(2,1)S(1)} fusion(bf16[2,2,2,480,16,128]{5,3,4,2,1,0:T(8,128)(2,1)} %copy-done.1, f32[2,2,16,480,32]{3,4,2,1,0:T(8,128)S(1)} %get-tuple-element.20, f32[2,2,16,32]{3,2,1,0:T(8,128)S(1)} %get-tuple-element.19, pred[2,2,480]{2,1,0:T(4,128)(4,1)S(1)} %broadcast_in_dim.36, f32[2,2,32,16]{2,3,1,0:T(8,128)S(1)} %bitcast.58), kind=kOutput, calls=%fused_computation.20 | convolution fusion | flops 256114688 | bytes 12339072 | tf_op jit(solution)/shard_map/tbhqk,tbkhe->tbqhe/dot_general | solution.py:72
  125.3 0.2 copy.44
  125.5 1.1 fusion.13
  126.6 0.0 all-reduce.3.cloned.1.call-update
  126.7 1.0 reshape.52
  127.7 53.4 %all-reduce.3.cloned.1.call-done = bf16[1,16,128,128]{3,2,1,0:T(8,128)(2,1)} async-done(((bf16[1,16,128,128]{3,2,1,0:T(8,128)(2,1)}), bf16[1,16,128,128]{3,2,1,0:T(8,128)(2,1)}) %all-reduce.3.cloned.1.call-update) | async-done | bytes 524304 | tf_op jit(solution)/shard_map/psum | solution.py:80
  181.0 2.1 %broadcast_in_dim.40 = f32[1,16,128,128]{3,2,1,0:T(8,128)} convert(bf16[1,16,128,128]{3,2,1,0:T(8,128)(2,1)} %all-reduce.3.cloned.1.call-done) | non-fusion elementwise | flops 262144 | bytes 1572864 | tf_op jit(solution)/shard_map/broadcast_in_dim | solution.py:81
  (6 shorter events, 0.0 us)
Async XLA Ops:
  7.2 25.8 %copy-start.3 = (s32[16]{0:T(128)S(1)}, s32[16]{0:T(128)}, u32[]{:S(2)}) copy-start(s32[16]{0:T(128)} %param.6) | copy-start | bytes 196
  7.2 26.9 %copy-start.2 = (s32[2,2,13]{2,1,0:T(2,128)S(1)}, s32[2,2,13]{2,1,0:T(2,128)}, u32[]{:S(2)}) copy-start(s32[2,2,13]{2,1,0:T(2,128)} %param.7) | copy-start | bytes 628
  7.2 173.9 %all-reduce.3.cloned.1.call-start = ((), (), s32[]{:S(2)}) async-start(), calls=%async_computation | async-start | bytes 1048576 | tf_op jit(solution)/shard_map/psum | solution.py:80
  7.2 16.6 %collective-permute-start = (bf16[2,2,64,2048]{3,2,1,0:T(8,128)(2,1)}, bf16[2,2,64,2048]{3,2,1,0:T(8,128)(2,1)S(1)}, u32[]{:S(2)}, u32[]{:S(2)}) collective-permute-start(bf16[2,2,64,2048]{3,2,1,0:T(8,128)(2,1)} %param.5), channel_id=1, source_target_pairs={{0,4},{4,8},{8,12},{12,16},{16,20},{20,24},{24,28},{1,5},{5,9},{9,... | collective-permute-start | bytes 3145736 | tf_op jit(solution)/shard_map/ppermute | solution.py:20
  11.8 16.7 %collective-permute-start.1 = (bf16[2,2,64,2048]{3,2,1,0:T(8,128)(2,1)}, bf16[2,2,64,2048]{3,2,1,0:T(8,128)(2,1)S(1)}, u32[]{:S(2)}, u32[]{:S(2)}) collective-permute-start(bf16[2,2,64,2048]{3,2,1,0:T(8,128)(2,1)} %param.5), channel_id=1, source_target_pairs={{4,0},{8,4},{12,8},{16,12},{20,16},{24,20},{28,24},{5,1},{9,5},{13... | collective-permute-start | bytes 3145736 | tf_op jit(solution)/shard_map/ppermute | solution.py:21
  30.5 37.4 %collective-permute-start.2 = (bf16[2,6,32,2048]{3,2,1,0:T(8,128)(2,1)}, bf16[2,6,32,2048]{3,2,1,0:T(8,128)(2,1)}, u32[]{:S(2)}, u32[]{:S(2)}) collective-permute-start(bf16[2,6,32,2048]{3,2,1,0:T(8,128)(2,1)} %get-tuple-element.17), channel_id=1, source_target_pairs={{0,1},{1,2},{2,3},{3,0},{4,5},{5,6},{6,7},{7,4},{8,9},{9,10},{10,1... | collective-permute-start | bytes 4718600 | tf_op jit(solution)/shard_map/ppermute | solution.py:28
  31.8 58.4 %collective-permute-start.3 = (bf16[2,6,32,2048]{3,2,1,0:T(8,128)(2,1)}, bf16[2,6,32,2048]{3,2,1,0:T(8,128)(2,1)}, u32[]{:S(2)}, u32[]{:S(2)}) collective-permute-start(bf16[2,6,32,2048]{3,2,1,0:T(8,128)(2,1)} %get-tuple-element.18), channel_id=1, source_target_pairs={{0,3},{1,0},{2,1},{3,2},{4,7},{5,4},{6,5},{7,6},{8,11},{9,8},{10,9... | collective-permute-start | bytes 4718600 | tf_op jit(solution)/shard_map/ppermute | solution.py:28
  104.2 8.0 %copy-start = (bf16[16,8,16,128]{3,2,1,0:T(8,128)(2,1)S(1)}, bf16[16,8,16,128]{3,2,1,0:T(8,128)(2,1)}, u32[]{:S(2)}) copy-start(bf16[16,8,16,128]{3,2,1,0:T(8,128)(2,1)} %copy.64) | copy-start | bytes 1572868
  106.7 5.5 %copy-start.1 = (bf16[2,2,2,480,16,128]{5,3,4,2,1,0:T(8,128)(2,1)}, bf16[2,2,2,480,16,128]{5,3,4,2,1,0:T(8,128)(2,1)S(1)}, u32[]{:S(2)}) copy-start(bf16[2,2,2,480,16,128]{5,3,4,2,1,0:T(8,128)(2,1)S(1)} %copy_dynamic-update-slice_fusion) | copy-start | bytes 47185924
Sparse Core Ops, SparseCore 0:
  126.8 54.2 all-reduce.2
where the time goes:
time: 191 us; the launch traced here: 190 us
  waiting for transfers between devices  121 us (63%)
  local copies, waits for them, and re-layouts  26.9 us (14%)
  between operations  14.3 us (7%)
  matrix products  12.9 us (7%)
  starting transfers between devices  8.92 us (5%)
  other arithmetic  6.37 us (3%)
    ppermute x2, waiting for transfers between devices, from_behind(): lax.ppermute(x, axis, [(i, (i + by) % length) for i in range(length)])  53.9 us
    psum x1, waiting for transfers between devices, local(): lax.psum(partial_value.astype(jnp.bfloat16), 'lon').astype(jnp.float32)  53.4 us
    unnamed x26, local copies, waits for them, and re-layouts  15.9 us
    ppermute x1, waiting for transfers between devices, extended(): before = lax.ppermute(last, axis, up)  10.1 us
    dot_general x1, matrix products, local(): jnp.einsum('tbqhe,tbkhe->tbhqk', qblocks, cand_band[0], preferred_element...  6.44 us
    slice x1, local copies, waits for them, and re-layouts, local(): wide_band[:, offset:offset + tile_rows, lon_step:lon_step + blocks]  6.23 us
    dot_general x1, matrix products, local(): jnp.einsum('tbhqk,tbkhe->tbqhe', rounded, cand_band[1], preferred_element...  5.31 us
    ppermute x1, starting transfers between devices, extended(): before = lax.ppermute(last, axis, up)  4.6 us
  transfers between devices with their start and end apart: 5, of which 5 were waited for; matrix products, arithmetic and copies ran while one was open for 3% of the time, Pallas kernels for 0%

commit v1 on v0

v1 whole, which is shorter than its diff:
```python
import functools
import math

import jax
import jax.numpy as jnp
from jax import lax
from jax.experimental import pallas as pl
from jax.experimental.pallas import tpu as pltpu
from jax.sharding import PartitionSpec as P

HEADS = 16
HD = 128
BLOCK = 32
HALO = 2
NB = 13
TLAT = 2
COLS = 64
GROUP = 2
NC = HEADS // GROUP
LANES = GROUP * HD
ROWS = TLAT + 2 * HALO
WIDE = COLS + 2 * BLOCK
KEYS = ROWS * WIDE
CELLS = TLAT * COLS
PACKED = HD + 16
AHEAD = 3
SCALE = HD ** (-0.5) * math.log2(math.e)
MESH = pl.DeviceIdType.MESH


def kernel(n_lat, n_lon, stages, q_hbm, kv_hbm, keep_ref, lists_ref, out_ref, gram_ref,
           ext, qs, bias, gsend, grecv,
           lon_send, lon_recv, own_send, own_recv, cor_send, cor_recv, gs_sem, gr_sem, loc_sem):
    lat = lax.axis_index("lat")
    lon = lax.axis_index("lon")
    west = lax.rem(lon + n_lon - 1, n_lon)
    east = lax.rem(lon + 1, n_lon)
    has_north = lat > 0
    has_south = lat < n_lat - 1
    partners = []
    for k in range(stages):
        bit = 1 << (stages - 1 - k)
        partners.append(lon + bit - 2 * bit * lax.rem(lon // bit, 2))

    barrier = pltpu.get_barrier_semaphore()
    for other in [west, east] + partners[:-1]:
        pl.semaphore_signal(barrier, inc=1, device_id=(lat, other), device_id_type=MESH)

    @pl.when(has_north)
    def _():
        pl.semaphore_signal(barrier, inc=1, device_id=(lat - 1, lon), device_id_type=MESH)

    @pl.when(has_south)
    def _():
        pl.semaphore_signal(barrier, inc=1, device_id=(lat + 1, lon), device_id_type=MESH)

    def lanes(c):
        return pl.ds(pl.multiple_of(c * LANES, LANES), LANES)

    def local_copies(c):
        return (
            pltpu.make_async_copy(
                kv_hbm.at[:, :, :, lanes(c)], ext.at[c, :, HALO : HALO + TLAT, 0:COLS], loc_sem.at[c, 0]
            ),
            pltpu.make_async_copy(q_hbm.at[:, :, lanes(c)], qs.at[c], loc_sem.at[c, 1]),
        )

    def local_start(c, carry):
        for copy in local_copies(c):
            copy.start()
        return carry

    lax.fori_loop(0, NC, local_start, 0)

    def remote(src, dst, send, recv, target):
        return pltpu.make_async_remote_copy(
            src_ref=src, dst_ref=dst, send_sem=send, recv_sem=recv, device_id=target, device_id_type=MESH
        )

    def to_west(c):
        return remote(
            kv_hbm.at[:, :, 0:BLOCK, lanes(c)],
            ext.at[c, :, HALO : HALO + TLAT, COLS + BLOCK : WIDE],
            lon_send.at[c, 0], lon_recv.at[c, 0], (lat, west),
        )

    def to_east(c):
        return remote(
            kv_hbm.at[:, :, COLS - BLOCK : COLS, lanes(c)],
            ext.at[c, :, HALO : HALO + TLAT, COLS : COLS + BLOCK],
            lon_send.at[c, 1], lon_recv.at[c, 1], (lat, east),
        )

    def own_north(c):
        return remote(
            kv_hbm.at[:, :, :, lanes(c)], ext.at[c, :, HALO + TLAT : ROWS, 0:COLS],
            own_send.at[c, 0], own_recv.at[c, 0], (lat - 1, lon),
        )

    def own_south(c):
        return remote(
            kv_hbm.at[:, :, :, lanes(c)], ext.at[c, :, 0:HALO, 0:COLS],
            own_send.at[c, 1], own_recv.at[c, 1], (lat + 1, lon),
        )

    def cor_north(c):
        return remote(
            ext.at[c, :, HALO : HALO + TLAT, COLS:WIDE], ext.at[c, :, HALO + TLAT : ROWS, COLS:WIDE],
            cor_send.at[c, 0], cor_recv.at[c, 0], (lat - 1, lon),
        )

    def cor_south(c):
        return remote(
            ext.at[c, :, HALO : HALO + TLAT, COLS:WIDE], ext.at[c, :, 0:HALO, COLS:WIDE],
            cor_send.at[c, 1], cor_recv.at[c, 1], (lat + 1, lon),
        )

    def gram_copy(k, c):
        return remote(
            gsend.at[k, c], grecv.at[k, c], gs_sem.at[k, c], gr_sem.at[k, c], (lat, partners[k])
        )

    def issue(c):
        to_west(c).start()
        to_east(c).start()

        @pl.when(has_north)
        def _():
            own_north(c).start()

        @pl.when(has_south)
        def _():
            own_south(c).start()

    pl.semaphore_wait(barrier, 1 + stages + has_north.astype(jnp.int32) + has_south.astype(jnp.int32))

    def first(c, carry):
        issue(c)
        return carry

    lax.fori_loop(0, min(AHEAD, NC), first, 0)

    @pl.when(jnp.logical_not(has_north))
    def _():
        def clear(c, carry):
            ext[c, :, 0:HALO] = jnp.zeros((2, HALO, WIDE, LANES), jnp.bfloat16)
            return carry
        lax.fori_loop(0, NC, clear, 0)

    @pl.when(jnp.logical_not(has_south))
    def _():
        def clear(c, carry):
            ext[c, :, HALO + TLAT : ROWS] = jnp.zeros((2, HALO, WIDE, LANES), jnp.bfloat16)
            return carry
        lax.fori_loop(0, NC, clear, 0)

    lane = lax.broadcasted_iota(jnp.int32, (8, KEYS), 1)
    row = lane // WIDE
    part = (lane - row * WIDE) // BLOCK
    total_rows = n_lat * TLAT
    kept = jnp.zeros((8, KEYS), jnp.int32)
    for e in range(ROWS):
        place = lat * TLAT - HALO + e
        flag = keep_ref[jnp.clip(place, 0, total_rows - 1)]
        kept = jnp.where(row == e, flag, kept)
    place = lat * TLAT - HALO + row
    inside = (place >= 0) & (place < total_rows)
    for t in range(TLAT):
        ok = inside & ((row == t + HALO) | (kept == 1)) & (row >= t) & (row <= t + 2 * HALO)
        for b in range(2):
            step = jnp.where(part == 0, 1 - b, jnp.where(part == 1, 2 - b, 0 if b == 0 else 2))
            ok_b = ok & (part != 3 - b)
            cand = 3 * (row - t) + step
            hit = cand == lists_ref[t, b, 0]
            for j in range(1, NB):
                hit = hit | (cand == lists_ref[t, b, j])
            value = jnp.where(ok_b & hit, 0.0, -jnp.inf).astype(jnp.float32)
            start = t * COLS + b * BLOCK
            for g in range(BLOCK // 8):
                bias[start + 8 * g : start + 8 * g + 8] = value

    ri = lax.broadcasted_iota(jnp.int32, (HD, HD), 0)
    ci = lax.broadcasted_iota(jnp.int32, (HD, HD), 1)

    def forward(c):
        to_west(c).wait_recv()
        to_east(c).wait_recv()

        @pl.when(has_north)
        def _():
            cor_north(c).start()

        @pl.when(has_south)
        def _():
            cor_south(c).start()

    def compute(c):
        for copy in local_copies(c):
            copy.wait()

        @pl.when(has_north)
        def _():
            own_south(c).wait_recv()
            cor_south(c).wait_recv()

        @pl.when(has_south)
        def _():
            own_north(c).wait_recv()
            cor_north(c).wait_recv()

        grams = []
        for g in range(GROUP):
            at = slice(g * HD, (g + 1) * HD)
            q = qs[c, :, :, at].reshape(CELLS, HD)
            k = ext[c, 0, :, :, at].reshape(KEYS, HD)
            v = ext[c, 1, :, :, at].reshape(KEYS, HD)
            s = lax.dot_general(q, k, (((1,), (1,)), ((), ())), preferred_element_type=jnp.float32)
            s = s + bias[...]
            top = jnp.max(s, axis=-1, keepdims=True)
            w = jnp.exp2((s - top) * SCALE)
            total = jnp.sum(w, axis=-1, keepdims=True)
            mix = jnp.dot(w.astype(jnp.bfloat16), v, preferred_element_type=jnp.float32)
            a = (mix / total).astype(jnp.bfloat16)
            out_ref[:, :, pl.ds(pl.multiple_of(c * LANES + g * HD, HD), HD)] = a.reshape(TLAT, COLS, HD)
            grams.append(
                lax.dot_general(a, a, (((0,), (0,)), ((), ())), preferred_element_type=jnp.float32)
            )
        g0, g1 = grams
        gsend[0, c, 0:HD] = jnp.where(ri <= ci, g0, g1).astype(jnp.bfloat16)
        diag = jnp.sum(jnp.where(ri == ci, g1, 0.0), axis=0, keepdims=True)
        gsend[0, c, HD:PACKED] = jnp.broadcast_to(diag, (PACKED - HD, HD)).astype(jnp.bfloat16)
        gram_copy(0, c).start()

    def gram_stage(k, c):
        gram_copy(k, c).wait_recv()
        both = gsend[k, c].astype(jnp.float32) + grecv[k, c].astype(jnp.float32)
        if k + 1 < stages:
            gsend[k + 1, c] = both.astype(jnp.bfloat16)
            gram_copy(k + 1, c).start()
        else:
            m = both[0:HD]
            mt = m.T
            d = jnp.broadcast_to(both[HD : HD + 1], (HD, HD))
            gram_ref[0, 2 * c] = jnp.where(ri <= ci, m, mt)
            gram_ref[0, 2 * c + 1] = jnp.where(ri > ci, m, jnp.where(ri == ci, d, mt))

    def step(s, carry):
        @pl.when(s + AHEAD < NC)
        def _():
            issue(s + AHEAD)

        @pl.when(s < NC)
        def _():
            forward(s)

        @pl.when((s >= 1) & (s <= NC))
        def _():
            compute(s - 1)

        for k in range(stages):
            @pl.when((s >= 2 + k) & (s < NC + 2 + k))
            def _():
                gram_stage(k, s - 2 - k)

        return carry

    lax.fori_loop(0, NC + 1 + stages, step, 0)

    def drain(c, carry):
        to_west(c).wait_send()
        to_east(c).wait_send()

        @pl.when(has_north)
        def _():
            own_north(c).wait_send()
            cor_north(c).wait_send()

        @pl.when(has_south)
        def _():
            own_south(c).wait_send()
            cor_south(c).wait_send()

        for k in range(stages):
            gram_copy(k, c).wait_send()
        return carry

    lax.fori_loop(0, NC, drain, 0)


def local(n_lat, n_lon, queries, keyval, keep, lists):
    stages = n_lon.bit_length() - 1
    assert n_lon == 1 << stages and queries.shape == (TLAT, COLS, HEADS * HD)
    dma = pltpu.SemaphoreType.DMA
    vmem = pl.BlockSpec(memory_space=pltpu.VMEM)
    smem = pl.BlockSpec(memory_space=pltpu.SMEM)
    hbm = pl.BlockSpec(memory_space=pl.ANY)
    return pl.pallas_call(
        functools.partial(kernel, n_lat, n_lon, stages),
        out_shape=(
            jax.ShapeDtypeStruct((TLAT, COLS, HEADS * HD), jnp.bfloat16),
            jax.ShapeDtypeStruct((1, HEADS, HD, HD), jnp.float32),
        ),
        in_specs=[hbm, hbm, smem, smem],
        out_specs=(vmem, vmem),
        scratch_shapes=[
            pltpu.VMEM((NC, 2, ROWS, WIDE, LANES), jnp.bfloat16),
            pltpu.VMEM((NC, TLAT, COLS, LANES), jnp.bfloat16),
            pltpu.VMEM((CELLS, KEYS), jnp.float32),
            pltpu.VMEM((stages, NC, PACKED, HD), jnp.bfloat16),
            pltpu.VMEM((stages, NC, PACKED, HD), jnp.bfloat16),
            dma((NC, 2)), dma((NC, 2)), dma((NC, 2)), dma((NC, 2)), dma((NC, 2)), dma((NC, 2)),
            dma((stages, NC)), dma((stages, NC)), dma((NC, 2)),
        ],
        compiler_params=pltpu.CompilerParams(
            collective_id=0, has_side_effects=True, vmem_limit_bytes=40 * 1024 * 1024
        ),
        cost_estimate=pl.CostEstimate(
            flops=4 * CELLS * KEYS * HEADS * HD, bytes_accessed=4 << 20, transcendentals=CELLS * KEYS * HEADS
        ),
    )(queries, keyval, keep, lists)


def solution(mesh):
    placed = (P("lat", "lon", None), P(None, "lat", "lon", None), P(), P("lat", "lon", None))
    return jax.shard_map(
        functools.partial(local, mesh.shape["lat"], mesh.shape["lon"]),
        mesh=mesh,
        in_specs=placed,
        out_specs=(P("lat", "lon", None), P("lat", None, None, None)),
        check_vma=False,
    )
```

time: 191 us -> 50.6 us (0.26)
  waiting for transfers between devices: 121 us -> 0 us
  Pallas kernels: 0 us -> 43.6 us
  local copies, waits for them, and re-layouts: 26.9 us -> 5.36 us
  between operations: 14.3 us -> 0.65 us
  matrix products: 12.9 us -> 0 us
  starting transfers between devices: 8.92 us -> 0 us
  other arithmetic: 6.37 us -> 0 us
    ppermute x4 -> x0, waiting for transfers between devices: 67.3 us -> none  [the longest x2 53.9 us: from_behind(): lax.ppermute(x, axis, [(i, (i + by) % length) for i in range(length)])]
    psum x1 -> x0, waiting for transfers between devices: 53.4 us -> none  [local(): lax.psum(partial_value.astype(jnp.bfloat16), 'lon').astype(jnp.float32)]
    pallas_call x0 -> x1, Pallas kernels: none -> 43.6 us  [local(): pl.pallas_call(functools.partial(kernel, n_lat, n_lon, stages), out_shape...]
    dot_general x3 -> x0, matrix products: 12.9 us -> none  [the longest x1 6.44 us: local(): jnp.einsum('tbqhe,tbkhe->tbhqk', qblocks, cand_band[0], preferred_element...]
    unnamed x26 -> x10, local copies, waits for them, and re-layouts: 15.9 us -> 5.36 us
    ppermute x4 -> x0, starting transfers between devices: 8.88 us -> none  [the longest x1 4.6 us: extended(): before = lax.ppermute(last, axis, up)]
    slice x2 -> x0, local copies, waits for them, and re-layouts: 8.11 us -> none  [the longest x1 6.23 us: local(): wide_band[:, offset:offset + tile_rows, lon_step:lon_step + blocks]]
    concatenate x1 -> x0, other arithmetic: 2.77 us -> none  [local(): wide_band = jnp.concatenate([west_keys, tall_band, east_keys], axis=2)]
  transfers between devices with their start and end apart: 5 -> 0, of which waited for: 5 -> 0; matrix products, arithmetic and copies ran while one was open for 3% -> 0% of each run, Pallas kernels for 0% -> 0%
where the time goes in v1:
time: 50.6 us; the launch traced here: 49.7 us
  Pallas kernels  43.6 us (86%)
  local copies, waits for them, and re-layouts  5.36 us (11%)
  between operations  0.65 us (1%)
    pallas_call x1, Pallas kernels, local(): pl.pallas_call(functools.partial(kernel, n_lat, n_lon, stages), out_shape...  43.6 us
    unnamed x10, local copies, waits for them, and re-layouts  5.36 us

profile of v1, /device:TPU:1, one launch (start us, length us, event | category | flops | bytes accessed | tf_op | source)
XLA Modules:
  0.0 49.7 jit_solution(16906804446269069001)
XLA Ops:
  0.6 0.0 copy-start
  0.6 1.2 %copy-done = bf16[2,2,64,2048]{3,2,1,0:T(8,128)(2,1)S(1)} copy-done((bf16[2,2,64,2048]{3,2,1,0:T(8,128)(2,1)S(1)}, bf16[2,2,64,2048]{3,2,1,0:T(8,128)(2,1)}, u32[]{:S(2)}) %copy-start) | copy-done | bytes 1048600
  1.9 0.0 copy-start.1
  1.9 1.0 %copy-done.1 = bf16[2,64,2048]{2,1,0:T(8,128)(2,1)S(1)} copy-done((bf16[2,64,2048]{2,1,0:T(8,128)(2,1)S(1)}, bf16[2,64,2048]{2,1,0:T(8,128)(2,1)}, u32[]{:S(2)}) %copy-start.1) | copy-done | bytes 524312
  2.9 0.0 copy-start.2
  2.9 0.7 %copy-done.2 = s32[2,2,13]{2,1,0:T(2,128)S(1)} copy-done((s32[2,2,13]{2,1,0:T(2,128)S(1)}, s32[2,2,13]{2,1,0:T(2,128)}, u32[]{:S(2)}) %copy-start.2) | copy-done | bytes 232
  3.6 0.0 copy-start.3
  3.6 0.7 %copy-done.3 = s32[16]{0:T(128)S(1)} copy-done((s32[16]{0:T(128)S(1)}, s32[16]{0:T(128)}, u32[]{:S(2)}) %copy-start.3) | copy-done | bytes 88
  4.2 43.6 %shard_map.59 = (bf16[2,64,2048]{2,1,0:T(8,128)(2,1)S(1)}, f32[1,16,128,128]{3,2,1,0:T(8,128)S(1)}) custom-call(bf16[2,64,2048]{2,1,0:T(8,128)(2,1)S(1)} %copy-done.1, bf16[2,2,64,2048]{3,2,1,0:T(8,128)(2,1)S(1)} %copy-done, s32[16]{0:T(128)S(1)} %copy-done.3, s32[2,2,13]{2,1,0:T(2,128)S(1)} %copy-done.2), custom_call_target="tpu_custom_call" | custom-call | flops 805306368 | bytes 4194304 | tf_op jit(solution)/shard_map/pallas_call | solution.py:297
  47.9 0.8 %copy.8 = bf16[2,64,2048]{2,1,0:T(8,128)(2,1)} copy(bf16[2,64,2048]{2,1,0:T(8,128)(2,1)S(1)} %get-tuple-element.4) | data formatting | bytes 1048576
  48.7 1.0 %copy.9 = f32[1,16,128,128]{3,2,1,0:T(8,128)} copy(f32[1,16,128,128]{3,2,1,0:T(8,128)S(1)} %get-tuple-element.5) | data formatting | bytes 2097152
Async XLA Ops:
  0.6 1.2 %copy-start = (bf16[2,2,64,2048]{3,2,1,0:T(8,128)(2,1)S(1)}, bf16[2,2,64,2048]{3,2,1,0:T(8,128)(2,1)}, u32[]{:S(2)}) copy-start(bf16[2,2,64,2048]{3,2,1,0:T(8,128)(2,1)} %kv_hbm.1) | copy-start | bytes 3145732
  1.9 1.0 %copy-start.1 = (bf16[2,64,2048]{2,1,0:T(8,128)(2,1)S(1)}, bf16[2,64,2048]{2,1,0:T(8,128)(2,1)}, u32[]{:S(2)}) copy-start(bf16[2,64,2048]{2,1,0:T(8,128)(2,1)} %q_hbm.1) | copy-start | bytes 1572868
  2.9 0.7 %copy-start.2 = (s32[2,2,13]{2,1,0:T(2,128)S(1)}, s32[2,2,13]{2,1,0:T(2,128)}, u32[]{:S(2)}) copy-start(s32[2,2,13]{2,1,0:T(2,128)} %lists_ref.1) | copy-start | bytes 628
  3.6 0.7 %copy-start.3 = (s32[16]{0:T(128)S(1)}, s32[16]{0:T(128)}, u32[]{:S(2)}) copy-start(s32[16]{0:T(128)} %keep_ref.1) | copy-start | bytes 196

commit v2 on v1

--- a/solution.py
+++ b/solution.py
@@ -23,14 +23,13 @@
 KEYS = ROWS * WIDE
 CELLS = TLAT * COLS
 PACKED = HD + 16
-AHEAD = 3
 SCALE = HD ** (-0.5) * math.log2(math.e)
 MESH = pl.DeviceIdType.MESH
 
 
-def kernel(n_lat, n_lon, stages, q_hbm, kv_hbm, keep_ref, lists_ref, out_ref, gram_ref,
-           ext, qs, bias, gsend, grecv,
-           lon_send, lon_recv, own_send, own_recv, cor_send, cor_recv, gs_sem, gr_sem, loc_sem):
+def kernel(n_lat, n_lon, stages, q_hbm, kv_hbm, keep_hbm, lists_hbm, out_ref, gram_ref,
+           keep_ref, lists_ref, ext, qs, bias, gsend, grecv,
+           lon_send, lon_recv, own_send, own_recv, cor_send, cor_recv, gs_sem, gr_sem, loc_sem, small_sem):
     lat = lax.axis_index("lat")
     lon = lax.axis_index("lon")
     west = lax.rem(lon + n_lon - 1, n_lon)
@@ -54,6 +53,11 @@
     def _():
         pl.semaphore_signal(barrier, inc=1, device_id=(lat + 1, lon), device_id_type=MESH)
 
+    keep_copy = pltpu.make_async_copy(keep_hbm, keep_ref, small_sem.at[0])
+    lists_copy = pltpu.make_async_copy(lists_hbm, lists_ref, small_sem.at[1])
+    keep_copy.start()
+    lists_copy.start()
+
     def lanes(c):
         return pl.ds(pl.multiple_of(c * LANES, LANES), LANES)
 
@@ -138,7 +142,7 @@
         issue(c)
         return carry
 
-    lax.fori_loop(0, min(AHEAD, NC), first, 0)
+    lax.fori_loop(0, NC, first, 0)
 
     @pl.when(jnp.logical_not(has_north))
     def _():
@@ -153,6 +157,9 @@
             ext[c, :, HALO + TLAT : ROWS] = jnp.zeros((2, HALO, WIDE, LANES), jnp.bfloat16)
             return carry
         lax.fori_loop(0, NC, clear, 0)
+
+    keep_copy.wait()
+    lists_copy.wait()
 
     lane = lax.broadcasted_iota(jnp.int32, (8, KEYS), 1)
     row = lane // WIDE
@@ -245,10 +252,6 @@
             gram_ref[0, 2 * c + 1] = jnp.where(ri > ci, m, jnp.where(ri == ci, d, mt))
 
     def step(s, carry):
-        @pl.when(s + AHEAD < NC)
-        def _():
-            issue(s + AHEAD)
-
         @pl.when(s < NC)
         def _():
             forward(s)
@@ -292,27 +295,28 @@
     assert n_lon == 1 << stages and queries.shape == (TLAT, COLS, HEADS * HD)
     dma = pltpu.SemaphoreType.DMA
     vmem = pl.BlockSpec(memory_space=pltpu.VMEM)
-    smem = pl.BlockSpec(memory_space=pltpu.SMEM)
-    hbm = pl.BlockSpec(memory_space=pl.ANY)
+    hbm = pl.BlockSpec(memory_space=pltpu.HBM)
     return pl.pallas_call(
         functools.partial(kernel, n_lat, n_lon, stages),
         out_shape=(
             jax.ShapeDtypeStruct((TLAT, COLS, HEADS * HD), jnp.bfloat16),
             jax.ShapeDtypeStruct((1, HEADS, HD, HD), jnp.float32),
         ),
-        in_specs=[hbm, hbm, smem, smem],
+        in_specs=[hbm] * 4,
         out_specs=(vmem, vmem),
         scratch_shapes=[
+            pltpu.SMEM(keep.shape, jnp.int32),
+            pltpu.SMEM(lists.shape, jnp.int32),
             pltpu.VMEM((NC, 2, ROWS, WIDE, LANES), jnp.bfloat16),
             pltpu.VMEM((NC, TLAT, COLS, LANES), jnp.bfloat16),
             pltpu.VMEM((CELLS, KEYS), jnp.float32),
             pltpu.VMEM((stages, NC, PACKED, HD), jnp.bfloat16),
             pltpu.VMEM((stages, NC, PACKED, HD), jnp.bfloat16),
             dma((NC, 2)), dma((NC, 2)), dma((NC, 2)), dma((NC, 2)), dma((NC, 2)), dma((NC, 2)),
-            dma((stages, NC)), dma((stages, NC)), dma((NC, 2)),
+            dma((stages, NC)), dma((stages, NC)), dma((NC, 2)), dma((2,)),
         ],
         compiler_params=pltpu.CompilerParams(
-            collective_id=0, has_side_effects=True, vmem_limit_bytes=40 * 1024 * 1024
+            collective_id=0, has_side_effects=True, vmem_limit_bytes=32 * 1024 * 1024
         ),
         cost_estimate=pl.CostEstimate(
             flops=4 * CELLS * KEYS * HEADS * HD, bytes_accessed=4 << 20, transcendentals=CELLS * KEYS * HEADS

time: 50.6 us -> 53.6 us (1.059); the launches traced: 49.7 us -> 53.4 us
  Pallas kernels: 43.6 us -> 47.4 us
    pallas_call x1, Pallas kernels: 43.6 us -> 47.4 us  [local(): pl.pallas_call(functools.partial(kernel, n_lat, n_lon, stages), out_shape...]
where the time goes in v2:
time: 53.6 us; the launch traced here: 53.4 us
  Pallas kernels  47.4 us (88%)
  local copies, waits for them, and re-layouts  5.36 us (10%)
  between operations  0.65 us (1%)
    pallas_call x1, Pallas kernels, local(): pl.pallas_call(functools.partial(kernel, n_lat, n_lon, stages), out_shape...  47.4 us
    unnamed x10, local copies, waits for them, and re-layouts  5.36 us

profile of v2, /device:TPU:1, one launch (start us, length us, event | category | flops | bytes accessed | tf_op | source)
XLA Modules:
  0.0 53.4 jit_solution(14611720098692083090)
XLA Ops:
  0.6 0.0 copy-start
  0.6 1.2 %copy-done = bf16[2,2,64,2048]{3,2,1,0:T(8,128)(2,1)S(1)} copy-done((bf16[2,2,64,2048]{3,2,1,0:T(8,128)(2,1)S(1)}, bf16[2,2,64,2048]{3,2,1,0:T(8,128)(2,1)}, u32[]{:S(2)}) %copy-start) | copy-done | bytes 1048600
  1.9 0.0 copy-start.1
  1.9 1.0 %copy-done.1 = bf16[2,64,2048]{2,1,0:T(8,128)(2,1)S(1)} copy-done((bf16[2,64,2048]{2,1,0:T(8,128)(2,1)S(1)}, bf16[2,64,2048]{2,1,0:T(8,128)(2,1)}, u32[]{:S(2)}) %copy-start.1) | copy-done | bytes 524312
  2.9 0.0 copy-start.2
  2.9 0.7 %copy-done.2 = s32[2,2,13]{2,1,0:T(2,128)S(1)} copy-done((s32[2,2,13]{2,1,0:T(2,128)S(1)}, s32[2,2,13]{2,1,0:T(2,128)}, u32[]{:S(2)}) %copy-start.2) | copy-done | bytes 232
  3.6 0.0 copy-start.3
  3.6 0.7 %copy-done.3 = s32[16]{0:T(128)S(1)} copy-done((s32[16]{0:T(128)S(1)}, s32[16]{0:T(128)}, u32[]{:S(2)}) %copy-start.3) | copy-done | bytes 88
  4.2 47.4 %shard_map.59 = (bf16[2,64,2048]{2,1,0:T(8,128)(2,1)S(1)}, f32[1,16,128,128]{3,2,1,0:T(8,128)S(1)}) custom-call(bf16[2,64,2048]{2,1,0:T(8,128)(2,1)S(1)} %copy-done.1, bf16[2,2,64,2048]{3,2,1,0:T(8,128)(2,1)S(1)} %copy-done, s32[16]{0:T(128)S(1)} %copy-done.3, s32[2,2,13]{2,1,0:T(2,128)S(1)} %copy-done.2), custom_call_target="tpu_custom_call" | custom-call | flops 805306368 | bytes 4194304 | tf_op jit(solution)/shard_map/pallas_call | solution.py:299
  51.6 0.8 %copy.8 = bf16[2,64,2048]{2,1,0:T(8,128)(2,1)} copy(bf16[2,64,2048]{2,1,0:T(8,128)(2,1)S(1)} %get-tuple-element.4) | data formatting | bytes 1048576
  52.4 1.0 %copy.9 = f32[1,16,128,128]{3,2,1,0:T(8,128)} copy(f32[1,16,128,128]{3,2,1,0:T(8,128)S(1)} %get-tuple-element.5) | data formatting | bytes 2097152
Async XLA Ops:
  0.6 1.2 %copy-start = (bf16[2,2,64,2048]{3,2,1,0:T(8,128)(2,1)S(1)}, bf16[2,2,64,2048]{3,2,1,0:T(8,128)(2,1)}, u32[]{:S(2)}) copy-start(bf16[2,2,64,2048]{3,2,1,0:T(8,128)(2,1)} %kv_hbm.1) | copy-start | bytes 3145732
  1.9 1.0 %copy-start.1 = (bf16[2,64,2048]{2,1,0:T(8,128)(2,1)S(1)}, bf16[2,64,2048]{2,1,0:T(8,128)(2,1)}, u32[]{:S(2)}) copy-start(bf16[2,64,2048]{2,1,0:T(8,128)(2,1)} %q_hbm.1) | copy-start | bytes 1572868
  2.9 0.7 %copy-start.2 = (s32[2,2,13]{2,1,0:T(2,128)S(1)}, s32[2,2,13]{2,1,0:T(2,128)}, u32[]{:S(2)}) copy-start(s32[2,2,13]{2,1,0:T(2,128)} %lists_hbm.1) | copy-start | bytes 628
  3.6 0.7 %copy-start.3 = (s32[16]{0:T(128)S(1)}, s32[16]{0:T(128)}, u32[]{:S(2)}) copy-start(s32[16]{0:T(128)} %keep_hbm.1) | copy-start | bytes 196

commit v3 on v2

--- a/solution.py
+++ b/solution.py
@@ -14,6 +14,7 @@
 HALO = 2
 NB = 13
 TLAT = 2
+AHEAD = 2
 COLS = 64
 GROUP = 2
 NC = HEADS // GROUP
@@ -142,7 +143,7 @@
         issue(c)
         return carry
 
-    lax.fori_loop(0, NC, first, 0)
+    lax.fori_loop(0, AHEAD, first, 0)
 
     @pl.when(jnp.logical_not(has_north))
     def _():
@@ -256,6 +257,10 @@
         def _():
             forward(s)
 
+        @pl.when(s + AHEAD < NC)
+        def _():
+            issue(s + AHEAD)
+
         @pl.when((s >= 1) & (s <= NC))
         def _():
             compute(s - 1)
@@ -299,8 +304,8 @@
     return pl.pallas_call(
         functools.partial(kernel, n_lat, n_lon, stages),
         out_shape=(
-            jax.ShapeDtypeStruct((TLAT, COLS, HEADS * HD), jnp.bfloat16),
-            jax.ShapeDtypeStruct((1, HEADS, HD, HD), jnp.float32),
+            pltpu.VMEM((TLAT, COLS, HEADS * HD), jnp.bfloat16),
+            pltpu.VMEM((1, HEADS, HD, HD), jnp.float32),
         ),
         in_specs=[hbm] * 4,
         out_specs=(vmem, vmem),
@@ -321,7 +326,7 @@
         cost_estimate=pl.CostEstimate(
             flops=4 * CELLS * KEYS * HEADS * HD, bytes_accessed=4 << 20, transcendentals=CELLS * KEYS * HEADS
         ),
-    )(queries, keyval, keep, lists)
+    )(*(pltpu.with_memory_space_constraint(x, pltpu.HBM) for x in (queries, keyval, keep, lists)))
 
 
 def solution(mesh):

time: 53.6 us -> 45.4 us (0.85)
  Pallas kernels: 47.4 us -> 42.8 us
  local copies, waits for them, and re-layouts: 5.36 us -> 1.77 us
    pallas_call x1, Pallas kernels: 47.4 us -> 42.8 us  [local(): pl.pallas_call(functools.partial(kernel, n_lat, n_lon, stages), out_shape...]
    unnamed x10 -> x2, local copies, waits for them, and re-layouts: 5.36 us -> 1.77 us
where the time goes in v3:
time: 45.4 us; the launch traced here: 45.2 us
  Pallas kernels  42.8 us (94%)
  local copies, waits for them, and re-layouts  1.77 us (4%)
  between operations  0.64 us (1%)
    pallas_call x1, Pallas kernels, local(): pl.pallas_call(functools.partial(kernel, n_lat, n_lon, stages), out_shape...  42.8 us
    unnamed x2, local copies, waits for them, and re-layouts  1.77 us

profile of v3, /device:TPU:1, one launch (start us, length us, event | category | flops | bytes accessed | tf_op | source)
XLA Modules:
  0.0 45.2 jit_solution(9122157173991248498)
XLA Ops:
  0.6 42.8 %shard_map.59 = (bf16[2,64,2048]{2,1,0:T(8,128)(2,1)S(1)}, f32[1,16,128,128]{3,2,1,0:T(8,128)S(1)}) custom-call(bf16[2,64,2048]{2,1,0:T(8,128)(2,1)} %q_hbm.1, bf16[2,2,64,2048]{3,2,1,0:T(8,128)(2,1)} %kv_hbm.1, s32[16]{0:T(128)} %keep_hbm.1, s32[2,2,13]{2,1,0:T(2,128)} %lists_hbm.1), custom_call_target="tpu_custom_call" | custom-call | flops 805306368 | bytes 4194304 | tf_op jit(solution)/shard_map/pallas_call | solution.py:304
  43.4 0.8 %copy.8 = bf16[2,64,2048]{2,1,0:T(8,128)(2,1)} copy(bf16[2,64,2048]{2,1,0:T(8,128)(2,1)S(1)} %get-tuple-element.2) | data formatting | bytes 1048576
  44.2 1.0 %copy.9 = f32[1,16,128,128]{3,2,1,0:T(8,128)} copy(f32[1,16,128,128]{3,2,1,0:T(8,128)S(1)} %get-tuple-element.3) | data formatting | bytes 2097152

commit v4 on v3

--- a/solution.py
+++ b/solution.py
@@ -14,7 +14,7 @@
 HALO = 2
 NB = 13
 TLAT = 2
-AHEAD = 2
+AHEAD = 4
 COLS = 64
 GROUP = 2
 NC = HEADS // GROUP
@@ -125,10 +125,11 @@
             gsend.at[k, c], grecv.at[k, c], gs_sem.at[k, c], gr_sem.at[k, c], (lat, partners[k])
         )
 
-    def issue(c):
+    def lon_issue(c):
         to_west(c).start()
         to_east(c).start()
 
+    def own_issue(c):
         @pl.when(has_north)
         def _():
             own_north(c).start()
@@ -140,10 +141,11 @@
     pl.semaphore_wait(barrier, 1 + stages + has_north.astype(jnp.int32) + has_south.astype(jnp.int32))
 
     def first(c, carry):
-        issue(c)
+        lon_issue(c)
         return carry
 
     lax.fori_loop(0, AHEAD, first, 0)
+    own_issue(0)
 
     @pl.when(jnp.logical_not(has_north))
     def _():
@@ -162,30 +164,33 @@
     keep_copy.wait()
     lists_copy.wait()
 
-    lane = lax.broadcasted_iota(jnp.int32, (8, KEYS), 1)
-    row = lane // WIDE
-    part = (lane - row * WIDE) // BLOCK
+    block = lax.broadcasted_iota(jnp.int32, (KEYS // BLOCK, CELLS), 0)
+    lane = lax.broadcasted_iota(jnp.int32, (KEYS // BLOCK, CELLS), 1)
+    row = block // (WIDE // BLOCK)
+    part = block - row * (WIDE // BLOCK)
+    t_of = lane // COLS
+    b_of = (lane - t_of * COLS) // BLOCK
     total_rows = n_lat * TLAT
-    kept = jnp.zeros((8, KEYS), jnp.int32)
+    kept = jnp.zeros_like(row)
     for e in range(ROWS):
         place = lat * TLAT - HALO + e
         flag = keep_ref[jnp.clip(place, 0, total_rows - 1)]
         kept = jnp.where(row == e, flag, kept)
     place = lat * TLAT - HALO + row
-    inside = (place >= 0) & (place < total_rows)
+    ok = (place >= 0) & (place < total_rows) & ((row == t_of + HALO) | (kept == 1))
+    ok = ok & (row >= t_of) & (row <= t_of + 2 * HALO) & (part != 3 - b_of)
+    step_lon = jnp.where(part < 2, part + 1 - b_of, 2 * b_of)
+    cand = 3 * (row - t_of) + step_lon
+    hit = jnp.zeros_like(row)
     for t in range(TLAT):
-        ok = inside & ((row == t + HALO) | (kept == 1)) & (row >= t) & (row <= t + 2 * HALO)
         for b in range(2):
-            step = jnp.where(part == 0, 1 - b, jnp.where(part == 1, 2 - b, 0 if b == 0 else 2))
-            ok_b = ok & (part != 3 - b)
-            cand = 3 * (row - t) + step
-            hit = cand == lists_ref[t, b, 0]
+            here = cand == lists_ref[t, b, 0]
             for j in range(1, NB):
-                hit = hit | (cand == lists_ref[t, b, j])
-            value = jnp.where(ok_b & hit, 0.0, -jnp.inf).astype(jnp.float32)
-            start = t * COLS + b * BLOCK
-            for g in range(BLOCK // 8):
-                bias[start + 8 * g : start + 8 * g + 8] = value
+                here = here | (cand == lists_ref[t, b, j])
+            hit = jnp.where(here & (t_of == t) & (b_of == b), 1, hit)
+    value = jnp.where(ok & (hit == 1), 0.0, -jnp.inf).astype(jnp.float32)
+    for n in range(KEYS // BLOCK):
+        bias[n] = jnp.broadcast_to(value[n : n + 1], (8, CELLS))
 
     ri = lax.broadcasted_iota(jnp.int32, (HD, HD), 0)
     ci = lax.broadcasted_iota(jnp.int32, (HD, HD), 1)
@@ -222,16 +227,20 @@
             q = qs[c, :, :, at].reshape(CELLS, HD)
             k = ext[c, 0, :, :, at].reshape(KEYS, HD)
             v = ext[c, 1, :, :, at].reshape(KEYS, HD)
-            s = lax.dot_general(q, k, (((1,), (1,)), ((), ())), preferred_element_type=jnp.float32)
-            s = s + bias[...]
-            top = jnp.max(s, axis=-1, keepdims=True)
+            s = lax.dot_general(k, q, (((1,), (1,)), ((), ())), preferred_element_type=jnp.float32)
+            s = s.reshape(KEYS // BLOCK, BLOCK // 8, 8, CELLS) + bias[...][:, None]
+            top = jnp.max(jnp.max(s, axis=(0, 1)), axis=0, keepdims=True)
             w = jnp.exp2((s - top) * SCALE)
-            total = jnp.sum(w, axis=-1, keepdims=True)
-            mix = jnp.dot(w.astype(jnp.bfloat16), v, preferred_element_type=jnp.float32)
-            a = (mix / total).astype(jnp.bfloat16)
-            out_ref[:, :, pl.ds(pl.multiple_of(c * LANES + g * HD, HD), HD)] = a.reshape(TLAT, COLS, HD)
+            total = jnp.sum(jnp.sum(w, axis=(0, 1)), axis=0, keepdims=True)
+            w = w.reshape(KEYS, CELLS).astype(jnp.bfloat16)
+            mix = lax.dot_general(v, w, (((0,), (0,)), ((), ())), preferred_element_type=jnp.float32)
+            mix = mix * (1.0 / total)
+            a = mix.astype(jnp.bfloat16)
+            out_ref[:, :, pl.ds(pl.multiple_of(c * LANES + g * HD, HD), HD)] = (
+                mix.T.astype(jnp.bfloat16).reshape(TLAT, COLS, HD)
+            )
             grams.append(
-                lax.dot_general(a, a, (((0,), (0,)), ((), ())), preferred_element_type=jnp.float32)
+                lax.dot_general(a, a, (((1,), (1,)), ((), ())), preferred_element_type=jnp.float32)
             )
         g0, g1 = grams
         gsend[0, c, 0:HD] = jnp.where(ri <= ci, g0, g1).astype(jnp.bfloat16)
@@ -259,7 +268,11 @@
 
         @pl.when(s + AHEAD < NC)
         def _():
-            issue(s + AHEAD)
+            lon_issue(s + AHEAD)
+
+        @pl.when(s + 1 < NC)
+        def _():
+            own_issue(s + 1)
 
         @pl.when((s >= 1) & (s <= NC))
         def _():
@@ -314,7 +327,7 @@
             pltpu.SMEM(lists.shape, jnp.int32),
             pltpu.VMEM((NC, 2, ROWS, WIDE, LANES), jnp.bfloat16),
             pltpu.VMEM((NC, TLAT, COLS, LANES), jnp.bfloat16),
-            pltpu.VMEM((CELLS, KEYS), jnp.float32),
+            pltpu.VMEM((KEYS // BLOCK, 8, CELLS), jnp.float32),
             pltpu.VMEM((stages, NC, PACKED, HD), jnp.bfloat16),
             pltpu.VMEM((stages, NC, PACKED, HD), jnp.bfloat16),
             dma((NC, 2)), dma((NC, 2)), dma((NC, 2)), dma((NC, 2)), dma((NC, 2)), dma((NC, 2)),

time: 45.4 us -> 48.9 us (1.077)
  Pallas kernels: 42.8 us -> 46.4 us
    pallas_call x1, Pallas kernels: 42.8 us -> 46.4 us  [local(): pl.pallas_call(functools.partial(kernel, n_lat, n_lon, stages), out_shape...]
where the time goes in v4:
time: 48.9 us; the launch traced here: 48.8 us
  Pallas kernels  46.4 us (95%)
  local copies, waits for them, and re-layouts  1.77 us (4%)
  between operations  0.64 us (1%)
    pallas_call x1, Pallas kernels, local(): pl.pallas_call(functools.partial(kernel, n_lat, n_lon, stages), out_shape...  46.4 us
    unnamed x2, local copies, waits for them, and re-layouts  1.77 us

profile of v4, /device:TPU:1, one launch (start us, length us, event | category | flops | bytes accessed | tf_op | source)
XLA Modules:
  0.0 48.8 jit_solution(5235747812458374450)
XLA Ops:
  0.6 46.4 %shard_map.59 = (bf16[2,64,2048]{2,1,0:T(8,128)(2,1)S(1)}, f32[1,16,128,128]{3,2,1,0:T(8,128)S(1)}) custom-call(bf16[2,64,2048]{2,1,0:T(8,128)(2,1)} %q_hbm.1, bf16[2,2,64,2048]{3,2,1,0:T(8,128)(2,1)} %kv_hbm.1, s32[16]{0:T(128)} %keep_hbm.1, s32[2,2,13]{2,1,0:T(2,128)} %lists_hbm.1), custom_call_target="tpu_custom_call" | custom-call | flops 805306368 | bytes 4194304 | tf_op jit(solution)/shard_map/pallas_call | solution.py:317
  47.0 0.8 %copy.8 = bf16[2,64,2048]{2,1,0:T(8,128)(2,1)} copy(bf16[2,64,2048]{2,1,0:T(8,128)(2,1)S(1)} %get-tuple-element.2) | data formatting | bytes 1048576
  47.8 1.0 %copy.9 = f32[1,16,128,128]{3,2,1,0:T(8,128)} copy(f32[1,16,128,128]{3,2,1,0:T(8,128)S(1)} %get-tuple-element.3) | data formatting | bytes 2097152

commit v5 on v4

--- a/solution.py
+++ b/solution.py
@@ -14,7 +14,7 @@
 HALO = 2
 NB = 13
 TLAT = 2
-AHEAD = 4
+AHEAD = 2
 COLS = 64
 GROUP = 2
 NC = HEADS // GROUP
@@ -142,10 +142,10 @@
 
     def first(c, carry):
         lon_issue(c)
+        own_issue(c)
         return carry
 
     lax.fori_loop(0, AHEAD, first, 0)
-    own_issue(0)
 
     @pl.when(jnp.logical_not(has_north))
     def _():
@@ -269,10 +269,7 @@
         @pl.when(s + AHEAD < NC)
         def _():
             lon_issue(s + AHEAD)
-
-        @pl.when(s + 1 < NC)
-        def _():
-            own_issue(s + 1)
+            own_issue(s + AHEAD)
 
         @pl.when((s >= 1) & (s <= NC))
         def _():

time: 48.9 us -> 45.3 us (0.926)
  Pallas kernels: 46.4 us -> 42.8 us
    pallas_call x1, Pallas kernels: 46.4 us -> 42.8 us  [local(): pl.pallas_call(functools.partial(kernel, n_lat, n_lon, stages), out_shape...]
where the time goes in v5:
time: 45.3 us; the launch traced here: 45.2 us
  Pallas kernels  42.8 us (94%)
  local copies, waits for them, and re-layouts  1.77 us (4%)
  between operations  0.64 us (1%)
    pallas_call x1, Pallas kernels, local(): pl.pallas_call(functools.partial(kernel, n_lat, n_lon, stages), out_shape...  42.8 us
    unnamed x2, local copies, waits for them, and re-layouts  1.77 us

profile of v5, /device:TPU:1, one launch (start us, length us, event | category | flops | bytes accessed | tf_op | source)
XLA Modules:
  0.0 45.2 jit_solution(10354442356281709590)
XLA Ops:
  0.6 42.8 %shard_map.59 = (bf16[2,64,2048]{2,1,0:T(8,128)(2,1)S(1)}, f32[1,16,128,128]{3,2,1,0:T(8,128)S(1)}) custom-call(bf16[2,64,2048]{2,1,0:T(8,128)(2,1)} %q_hbm.1, bf16[2,2,64,2048]{3,2,1,0:T(8,128)(2,1)} %kv_hbm.1, s32[16]{0:T(128)} %keep_hbm.1, s32[2,2,13]{2,1,0:T(2,128)} %lists_hbm.1), custom_call_target="tpu_custom_call" | custom-call | flops 805306368 | bytes 4194304 | tf_op jit(solution)/shard_map/pallas_call | solution.py:314
  43.4 0.8 %copy.8 = bf16[2,64,2048]{2,1,0:T(8,128)(2,1)} copy(bf16[2,64,2048]{2,1,0:T(8,128)(2,1)S(1)} %get-tuple-element.2) | data formatting | bytes 1048576
  44.2 1.0 %copy.9 = f32[1,16,128,128]{3,2,1,0:T(8,128)} copy(f32[1,16,128,128]{3,2,1,0:T(8,128)S(1)} %get-tuple-element.3) | data formatting | bytes 2097152

commit v6 on v5

--- a/solution.py
+++ b/solution.py
@@ -271,18 +271,18 @@
             lon_issue(s + AHEAD)
             own_issue(s + AHEAD)
 
-        @pl.when((s >= 1) & (s <= NC))
-        def _():
-            compute(s - 1)
+        @pl.when((s >= 2) & (s < NC + 2))
+        def _():
+            compute(s - 2)
 
         for k in range(stages):
-            @pl.when((s >= 2 + k) & (s < NC + 2 + k))
+            @pl.when((s >= 4 + k) & (s < NC + 4 + k))
             def _():
-                gram_stage(k, s - 2 - k)
+                gram_stage(k, s - 4 - k)
 
         return carry
 
-    lax.fori_loop(0, NC + 1 + stages, step, 0)
+    lax.fori_loop(0, NC + 3 + stages, step, 0)
 
     def drain(c, carry):
         to_west(c).wait_send()

time: 45.3 us -> 45.6 us (level)
  the two profiles are of different devices: /device:TPU:1 before, /device:TPU:0 now
where the time goes in v6:
time: 45.6 us; the launch traced here: 45.5 us
  Pallas kernels  43.1 us (95%)
  local copies, waits for them, and re-layouts  1.77 us (4%)
  between operations  0.64 us (1%)
    pallas_call x1, Pallas kernels, local(): pl.pallas_call(functools.partial(kernel, n_lat, n_lon, stages), out_shape...  43.1 us
    unnamed x2, local copies, waits for them, and re-layouts  1.77 us

profile of v6, /device:TPU:0, one launch (start us, length us, event | category | flops | bytes accessed | tf_op | source)
XLA Modules:
  0.0 45.5 jit_solution(14309649517735276312)
XLA Ops:
  0.6 43.1 %shard_map.59 = (bf16[2,64,2048]{2,1,0:T(8,128)(2,1)S(1)}, f32[1,16,128,128]{3,2,1,0:T(8,128)S(1)}) custom-call(bf16[2,64,2048]{2,1,0:T(8,128)(2,1)} %q_hbm.1, bf16[2,2,64,2048]{3,2,1,0:T(8,128)(2,1)} %kv_hbm.1, s32[16]{0:T(128)} %keep_hbm.1, s32[2,2,13]{2,1,0:T(2,128)} %lists_hbm.1), custom_call_target="tpu_custom_call" | custom-call | flops 805306368 | bytes 4194304 | tf_op jit(solution)/shard_map/pallas_call | solution.py:314
  43.7 0.8 %copy.8 = bf16[2,64,2048]{2,1,0:T(8,128)(2,1)} copy(bf16[2,64,2048]{2,1,0:T(8,128)(2,1)S(1)} %get-tuple-element.2) | data formatting | bytes 1048576
  44.5 1.0 %copy.9 = f32[1,16,128,128]{3,2,1,0:T(8,128)} copy(f32[1,16,128,128]{3,2,1,0:T(8,128)S(1)} %get-tuple-element.3) | data formatting | bytes 2097152
